TPU v7x, 32 devices: a whole 2x2x4 slice. The times are simulated.
32 devices in a mesh: grp: 4 (over y, core), tile: 8 (over z, x).
Axes of the slice: x: 2, y: 2, z: 4, core: 2. Of those that a mesh axis runs over, the one named last changes fastest.
Arguments:
- adjoint_state: float32 [64, 128, 2048], P('tile', 'grp'), may hold values from -6 to 6
- misfit: float32 [64, 128, 2048], P('tile', 'grp'), may hold values from -4 to 4
- east_speed: float32 [64, 128, 2048], P('tile', 'grp'), may hold values from -0.6 to 0.6
- north_speed: float32 [64, 128, 2048], P('tile', 'grp'), may hold values from -0.6 to 0.6
- land_mask: int32 [64, 128, 2048], P('tile', 'grp'), may hold values 0 or 1
- warming_forcing_selector: int32 [128, 2048], P('grp', 'tile'), may hold values 0 or 1
- vertical_filter_matrix: float32 [64, 64], replicated, may hold values from 0 to 0.54
Outputs:
- filtered_thermal_sensitivity: float32 [64, 128, 2048], P('tile', 'grp')
- boundary_warming_sensitivity: float32 [128, 2048], P('grp', 'tile')
All inputs are finite; a program needn't handle non-finite values. No bound on the sum of `land_mask` or of `warming_forcing_selector` on one device may be relied on, other than what follows from the above.
Results may differ from a plain program's by a relative error of at most 0.000088.
Values sent between devices are 32-bit elements; how exact they have to be, the bound alone decides.
A program may use at most 192 MiB of HBM per device.

v0:
```python
import functools

import jax
import jax.numpy as jnp
from jax import lax
from jax.experimental import pallas as pl
from jax.experimental.pallas import tpu as pltpu
from jax.sharding import PartitionSpec as P

MESH = pl.DeviceIdType.MESH
SUB = 8
LANE = 128
WIDTH = 512
SIDE = 256
HIGHEST = lax.Precision.HIGHEST


def kernel(
    tiles,
    grps,
    state_ref,
    misfit_ref,
    east_ref,
    north_ref,
    land_ref,
    select_ref,
    matrix_ref,
    out_ref,
    surface_ref,
    s0,
    s1,
    s2,
    misfit,
    east,
    north,
    land,
    pencil,
    smooth,
    kron,
    matrix,
    select,
    load_sem,
    level_send,
    level_recv,
    row_send,
    row_recv,
    fwd_send,
    fwd_recv,
    ret_send,
    ret_recv,
):
    levels, rows, columns = state_ref.shape
    chunks = rows // SUB
    part = columns // tiles
    half = tiles // 2
    mine = columns // 2
    near = min(2, levels // 2)
    tile = lax.axis_index("tile")
    grp = lax.axis_index("grp")
    side = lax.div(tile, half)
    inner = (pl.ds(SUB, rows), pl.ds(LANE, columns))

    far_at = pl.multiple_of((1 - side) * mine, LANE)
    near_at = pl.multiple_of(side * mine, LANE)
    first_at = pl.multiple_of((1 - side) * (mine - SIDE), LANE)
    then_at = pl.multiple_of(side * (mine + SIDE), LANE)
    first_width, then_width = mine + SIDE, mine - SIDE

    def load(ref, buf, at, width, k):
        span = pl.ds(at, width)
        return pltpu.make_async_copy(ref.at[:, :, span], buf.at[:, :, span], load_sem.at[k])

    tracer = pltpu.make_async_copy(
        state_ref, s0.at[(pl.ds(1, levels),) + inner], load_sem.at[0]
    )
    fields = ((misfit_ref, misfit), (east_ref, east), (north_ref, north), (land_ref, land))
    loads = [tracer] + [
        load(ref, buf, first_at, first_width, 1 + k) for k, (ref, buf) in enumerate(fields)
    ]
    later = [load(ref, buf, then_at, then_width, 5 + k) for k, (ref, buf) in enumerate(fields)]
    small = [
        pltpu.make_async_copy(matrix_ref, matrix, load_sem.at[9]),
        pltpu.make_async_copy(select_ref, select, load_sem.at[10]),
    ]

    barrier = pltpu.get_barrier_semaphore()

    @pl.loop(1, tiles)
    def _(i):
        other = lax.rem(tile + i, tiles)
        pl.semaphore_signal(barrier, inc=1, device_id=(grp, other), device_id_type=MESH)

    @pl.when(grp > 0)
    def _():
        pl.semaphore_signal(barrier, inc=1, device_id=(grp - 1, tile), device_id_type=MESH)

    @pl.when(grp < grps - 1)
    def _():
        pl.semaphore_signal(barrier, inc=1, device_id=(grp + 1, tile), device_id_type=MESH)

    for copy in loads + later + small:
        copy.start()

    for buf in (s0, s1):
        for start in (0, columns + LANE):
            buf[1 : levels + 1, SUB : SUB + rows, start : start + LANE] = jnp.zeros(
                (levels, rows, LANE), jnp.float32
            )

        @pl.when(tile == 0)
        def _():
            buf[0, SUB : SUB + rows, :] = jnp.zeros((rows, columns + 2 * LANE), jnp.float32)

        @pl.when(tile == tiles - 1)
        def _():
            buf[levels + 1, SUB : SUB + rows, :] = jnp.zeros((rows, columns + 2 * LANE), jnp.float32)

        @pl.when(grp == 0)
        def _():
            buf[1 : levels + 1, 0:SUB, :] = jnp.zeros((levels, SUB, columns + 2 * LANE), jnp.float32)

        @pl.when(grp == grps - 1)
        def _():
            buf[1 : levels + 1, SUB + rows :, :] = jnp.zeros(
                (levels, SUB, columns + 2 * LANE), jnp.float32
            )

    beside = (grp > 0).astype(jnp.int32) + (grp < grps - 1).astype(jnp.int32)

    def level_copies(buf, step):
        top, bottom = state_ref.at[0], state_ref.at[levels - 1]
        if step:
            top, bottom = buf.at[(1,) + inner], buf.at[(levels,) + inner]
        return [
            (
                tile > 0,
                tile < tiles - 1,
                pltpu.make_async_remote_copy(
                    top,
                    buf.at[(levels + 1,) + inner],
                    level_send.at[step, 0],
                    level_recv.at[step, 0],
                    (grp, tile - 1),
                    MESH,
                ),
            ),
            (
                tile < tiles - 1,
                tile > 0,
                pltpu.make_async_remote_copy(
                    bottom,
                    buf.at[(0,) + inner],
                    level_send.at[step, 1],
                    level_recv.at[step, 1],
                    (grp, tile + 1),
                    MESH,
                ),
            ),
        ]

    def row_copies(buf, step, slot, first, count):
        span = pl.ds(first + 1, count)
        across = pl.ds(LANE, columns)
        top, bottom = state_ref.at[:, pl.ds(0, 1), :], state_ref.at[:, pl.ds(rows - 1, 1), :]
        if step:
            top = buf.at[span, pl.ds(SUB, 1), across]
            bottom = buf.at[span, pl.ds(SUB + rows - 1, 1), across]
        return [
            (
                grp > 0,
                grp < grps - 1,
                pltpu.make_async_remote_copy(
                    top,
                    buf.at[span, pl.ds(SUB + rows, 1), across],
                    row_send.at[slot, 0],
                    row_recv.at[slot, 0],
                    (grp - 1, tile),
                    MESH,
                ),
            ),
            (
                grp < grps - 1,
                grp > 0,
                pltpu.make_async_remote_copy(
                    bottom,
                    buf.at[span, pl.ds(SUB - 1, 1), across],
                    row_send.at[slot, 1],
                    row_recv.at[slot, 1],
                    (grp + 1, tile),
                    MESH,
                ),
            ),
        ]

    def start(copies):
        for sends, _, copy in copies:
            pl.when(sends)(copy.start)

    def arrive(copies):
        for _, receives, copy in copies:
            pl.when(receives)(copy.wait_recv)

    def leave(copies):
        for sends, _, copy in copies:
            pl.when(sends)(copy.wait_send)

    def advance(src, dst, pad, first, count, row_first, row_count, at, width, edge=0):
        if count <= 0 or row_count <= 0:
            return
        pieces = [(k, min(WIDTH, width - k)) for k in range(0, width, WIDTH)]

        @pl.loop(0, count * row_count)
        def _(i):
            level = first + lax.div(i, row_count)
            row = pl.multiple_of((row_first + lax.rem(i, row_count)) * SUB, SUB)
            rr = pl.ds(row, SUB)
            middle = pl.ds(row + SUB, SUB)
            for k, wide_by in pieces:
                here = pl.ds(pl.multiple_of(at + k, LANE), wide_by)
                mid = pl.ds(pl.multiple_of(at + k + LANE, LANE), wide_by)
                around = wide_by + 2 * LANE
                wide = src[level + 1, middle, pl.ds(pl.multiple_of(at + k, LANE), around)]
                center = wide[:, LANE : LANE + wide_by]
                e = pltpu.roll(wide, around - 1, 1)[:, LANE : LANE + wide_by]
                w = pltpu.roll(wide, 1, 1)[:, LANE : LANE + wide_by]
                index = lax.broadcasted_iota(jnp.int32, (SUB, wide_by), 0)
                n, s = center, center
                if edge <= 0:
                    down = src[level + 1, pl.ds(row + 2 * SUB, SUB), mid]
                    n = jnp.where(index == 0, down, center)
                if edge >= 0:
                    up = src[level + 1, pl.ds(row, SUB), mid]
                    s = jnp.where(index == SUB - 1, up, center)
                n = pltpu.roll(n, SUB - 1, 0)
                s = pltpu.roll(s, 1, 0)
                a = src[level, middle, mid]
                b = src[level + 2, middle, mid]
                flow = east[level, rr, here] * (e - w) + north[level, rr, here] * (n - s)
                value = (
                    (0.3 * center + misfit[level, rr, here])
                    + 0.5 * flow
                    + (0.1 * ((e + w) + (n + s)) + 0.15 * (a + b))
                )
                value = land[level, rr, here].astype(jnp.float32) * value
                if pad:
                    dst[level + 1, middle, mid] = value
                else:
                    dst[level, rr, here] = value

    def forward(first, count, row_first, row_count, far):
        if count <= 0:
            return
        here = lax.rem(tile, half)
        base = (1 - side) * half if far else side * half
        for r in range(row_first, row_first + row_count):
            span = pl.ds(r * SUB, SUB)
            target = pencil.at[pl.ds(tile * levels + first, count), span, :]

            @pl.loop(0 if far else 1, half)
            def _(i):
                other = base + lax.rem(here + i, half)
                cut = pl.ds(pl.multiple_of(other * part, LANE), part)
                pltpu.make_async_remote_copy(
                    s2.at[pl.ds(first, count), span, cut],
                    target,
                    fwd_send,
                    fwd_recv.at[r],
                    (grp, other),
                    MESH,
                ).start()

            if not far:
                own = pl.ds(pl.multiple_of(tile * part, LANE), part)
                pltpu.make_async_copy(
                    s2.at[pl.ds(first, count), span, own], target, fwd_recv.at[r]
                ).start()

    early = levels - 2 * near
    inside = levels - 2
    far_part, near_part = (far_at, mine), (near_at, mine)
    first_part, then_part = (first_at, first_width), (then_at, then_width)
    every = (0, columns)

    for copy in loads:
        copy.wait()
    advance(s0, s1, True, 1, inside, 0, 1, *first_part, edge=-1)
    advance(s0, s1, True, 1, inside, 1, chunks - 2, *first_part)
    advance(s0, s1, True, 1, inside, chunks - 1, 1, *first_part, edge=1)
    advance(s1, s2, False, near, early, 1, chunks - 2, *far_part)

    pl.semaphore_wait(barrier, tiles - 1 + beside)

    level0 = level_copies(s0, 0)
    row0 = row_copies(s0, 0, 0, 0, levels)
    start(row0)
    start(level0)
    forward(near, early, 1, chunks - 2, True)

    for copy in later + small:
        copy.wait()
    advance(s0, s1, True, 1, inside, 1, chunks - 2, *then_part)
    arrive(row0)
    advance(s0, s1, True, 1, inside, 0, 1, *every)
    advance(s0, s1, True, 1, inside, chunks - 1, 1, *every)
    level1 = level_copies(s1, 1)
    row_mid = row_copies(s1, 1, 1, 1, levels - 2) if levels > 2 else []
    row_ends = row_copies(s1, 1, 2, 0, 1) + row_copies(s1, 1, 3, levels - 1, 1)
    start(row_mid)
    advance(s1, s2, False, near, early, 1, chunks - 2, *near_part)
    forward(near, early, 1, chunks - 2, False)

    arrive(level0)
    advance(s0, s1, True, 0, 1, 0, chunks, *every)
    advance(s0, s1, True, levels - 1, 1, 0, chunks, *every)
    start(level1)
    start(row_ends)

    arrive(row_mid)
    for r in (0, chunks - 1):
        advance(s1, s2, False, near, early, r, 1, *every)
    for r in (0, chunks - 1):
        forward(near, early, r, 1, True)
        forward(near, early, r, 1, False)
    advance(s1, s2, False, 1, near - 1, 0, chunks, *every)
    advance(s1, s2, False, levels - near, near - 1, 0, chunks, *every)

    size = tiles * levels * SUB
    repeat = (
        lax.shift_right_logical(lax.broadcasted_iota(jnp.int32, (size, tiles * levels), 0), 3)
        == lax.broadcasted_iota(jnp.int32, (size, tiles * levels), 1)
    ).astype(jnp.float32)
    tall = jnp.dot(repeat, matrix[...], precision=HIGHEST, preferred_element_type=jnp.float32)
    full = lax.dot_general(
        tall,
        repeat,
        (((1,), (1,)), ((), ())),
        precision=HIGHEST,
        preferred_element_type=jnp.float32,
    )
    same = (lax.broadcasted_iota(jnp.int32, (size, size), 0) & (SUB - 1)) == (
        lax.broadcasted_iota(jnp.int32, (size, size), 1) & (SUB - 1)
    )
    kron[...] = jnp.where(same, full, 0.0)

    arrive(level1)
    arrive(row_ends)
    order = list(range(1, chunks - 1)) + [0, chunks - 1]
    for r in order:
        advance(s1, s2, False, 0, 1, r, 1, *every)
        advance(s1, s2, False, levels - 1, 1, r, 1, *every)
        for far in (True, False):
            forward(0, near, r, 1, far)
            forward(levels - near, near, r, 1, far)

    for r in order:
        span = pl.ds(r * SUB, SUB)
        chunk = pencil.at[:, span, :]
        pltpu.make_async_copy(chunk, chunk, fwd_recv.at[r]).wait()
        result = jnp.dot(
            kron[...],
            pencil[:, r * SUB : (r + 1) * SUB, :].reshape(size, part),
            precision=HIGHEST,
            preferred_element_type=jnp.float32,
        )
        smooth[:, r * SUB : (r + 1) * SUB, :] = result.reshape(tiles * levels, SUB, part)
        home = out_ref.at[:, span, pl.ds(pl.multiple_of(tile * part, LANE), part)]

        def give(other):
            pltpu.make_async_remote_copy(
                smooth.at[pl.ds(other * levels, levels), span, :],
                home,
                ret_send,
                ret_recv,
                (grp, other),
                MESH,
            ).start()

        @pl.loop(0, half)
        def _(i):
            give((1 - side) * half + i)

        @pl.loop(1, half)
        def _(i):
            give(side * half + lax.rem(lax.rem(tile, half) + i, half))

        pltpu.make_async_copy(
            smooth.at[pl.ds(tile * levels, levels), span, :], home, ret_recv
        ).start()
        surface_ref[r * SUB : (r + 1) * SUB, :] = (
            select[r * SUB : (r + 1) * SUB, :].astype(jnp.float32) * result[0:SUB]
        )

    for copies in (level0, row0, level1, row_mid, row_ends):
        leave(copies)
    sent = s2.at[:, :, pl.ds(0, (tiles - 1) * part)]
    pltpu.make_async_copy(sent, sent, fwd_send).wait()
    returned = smooth.at[pl.ds(0, (tiles - 1) * levels)]
    pltpu.make_async_copy(returned, returned, ret_send).wait()
    pltpu.make_async_copy(out_ref, out_ref, ret_recv).wait()


def body(tiles, grps, *args):
    levels, rows, columns = args[0].shape
    part = columns // tiles
    total = tiles * levels
    padded = (levels + 2, rows + 2 * SUB, columns + 2 * LANE)
    block = (levels, rows, columns)
    hbm = pl.BlockSpec(memory_space=pltpu.HBM)
    vmem = pl.BlockSpec(memory_space=pltpu.VMEM)
    return pl.pallas_call(
        functools.partial(kernel, tiles, grps),
        out_shape=(
            pltpu.VMEM(block, jnp.float32),
            pltpu.VMEM((rows, part), jnp.float32),
        ),
        in_specs=[hbm] * 7,
        out_specs=(vmem, vmem),
        scratch_shapes=[
            pltpu.VMEM(padded, jnp.float32),
            pltpu.VMEM(padded, jnp.float32),
            pltpu.VMEM(block, jnp.float32),
            pltpu.VMEM(block, jnp.float32),
            pltpu.VMEM(block, jnp.float32),
            pltpu.VMEM(block, jnp.float32),
            pltpu.VMEM(block, jnp.int32),
            pltpu.VMEM((total, rows, part), jnp.float32),
            pltpu.VMEM((total, rows, part), jnp.float32),
            pltpu.VMEM((total * SUB, total * SUB), jnp.float32),
            pltpu.VMEM((total, total), jnp.float32),
            pltpu.VMEM((rows, part), jnp.int32),
            pltpu.SemaphoreType.DMA((11,)),
            pltpu.SemaphoreType.DMA((2, 2)),
            pltpu.SemaphoreType.DMA((2, 2)),
            pltpu.SemaphoreType.DMA((4, 2)),
            pltpu.SemaphoreType.DMA((4, 2)),
            pltpu.SemaphoreType.DMA,
            pltpu.SemaphoreType.DMA((rows // SUB,)),
            pltpu.SemaphoreType.DMA,
            pltpu.SemaphoreType.DMA,
        ],
        compiler_params=pltpu.CompilerParams(
            collective_id=0, has_side_effects=True, vmem_limit_bytes=40 * 1024 * 1024
        ),
    )(*[pltpu.with_memory_space_constraint(arg, pltpu.HBM) for arg in args])


def solution(mesh):
    split = P("tile", "grp", None)
    return jax.shard_map(
        functools.partial(body, mesh.shape["tile"], mesh.shape["grp"]),
        mesh=mesh,
        in_specs=(split,) * 5 + (P("grp", "tile"), P()),
        out_specs=(split, P("grp", "tile")),
        check_vma=False,
    )
```

profile of v0, /device:TPU:10, one launch (start us, length us, event | category | flops | bytes accessed | tf_op | source)
XLA Modules:
  0.0 115.4 jit_solution(3846418397889627485)
XLA Ops:
  0.6 112.8 %shard_map.86 = (f32[8,32,2048]{2,1,0:T(8,128)S(1)}, f32[32,256]{1,0:T(8,128)S(1)}) custom-call(f32[8,32,2048]{2,1,0:T(8,128)} %state_ref.1, f32[8,32,2048]{2,1,0:T(8,128)} %misfit_ref.1, f32[8,32,2048]{2,1,0:T(8,128)} %east_ref.1, f32[8,32,2048]{2,1,0:T(8,128)} %north_ref.1, s32[8,32,2048]{2,1,0:T(8,128)} %land_ref.1, s32[32,256]{1,0:T(8,128)} %select_ref.1, ...), custom_call_target="tpu_custom_call" | custom-call | tf_op jit(solution)/shard_map/pallas_call | solution.py:410
  113.5 1.3 %copy.11 = f32[8,32,2048]{2,1,0:T(8,128)} copy(f32[8,32,2048]{2,1,0:T(8,128)S(1)} %get-tuple-element.2) | data formatting | bytes 4194304
  114.8 0.6 copy.12
where the time goes:
time: 117 us; the launch traced here: 115 us
  Pallas kernels  113 us (97%)
  local copies, waits for them, and re-layouts  1.94 us (2%)
    pallas_call x1, Pallas kernels, body(): pl.pallas_call(functools.partial(kernel, tiles, grps), out_shape=(pltpu.V...  113 us

commit v1 on v0

--- a/solution.py
+++ b/solution.py
@@ -11,7 +11,6 @@
 SUB = 8
 LANE = 128
 WIDTH = 512
-SIDE = 256
 HIGHEST = lax.Precision.HIGHEST
 
 
@@ -39,6 +38,9 @@
     kron,
     matrix,
     select,
+    pencil_u,
+    smooth_u,
+    border,
     load_sem,
     level_send,
     level_recv,
@@ -48,6 +50,7 @@
     fwd_recv,
     ret_send,
     ret_recv,
+    border_sem,
 ):
     levels, rows, columns = state_ref.shape
     chunks = rows // SUB
@@ -58,13 +61,38 @@
     tile = lax.axis_index("tile")
     grp = lax.axis_index("grp")
     side = lax.div(tile, half)
+    uneven = 0
+    widths = (part + LANE, part - LANE)
+    wide_here = lax.rem(tile, 2) == side
+    partner = tile + 1 - 2 * lax.rem(tile, 2)
+
+    def uneven_start(other):
+        odd = lax.rem(other, 2)
+        shift = odd * (1 - 2 * lax.div(other, half)) * LANE
+        return pl.multiple_of(other * part + shift, LANE)
+
+    def by_width(other, run):
+        wide = lax.rem(other, 2) == lax.div(other, half)
+        pl.when(wide)(lambda: run(widths[0]))
+        pl.when(jnp.logical_not(wide))(lambda: run(widths[1]))
     inner = (pl.ds(SUB, rows), pl.ds(LANE, columns))
 
-    far_at = pl.multiple_of((1 - side) * mine, LANE)
-    near_at = pl.multiple_of(side * mine, LANE)
-    first_at = pl.multiple_of((1 - side) * (mine - SIDE), LANE)
-    then_at = pl.multiple_of(side * (mine + SIDE), LANE)
-    first_width, then_width = mine + SIDE, mine - SIDE
+    early = levels - 2 * near
+    inside = levels - 2
+    pair = 2 * part
+    pairs = half // 2
+    parity = lax.rem(tile, 2)
+    light = parity == side
+    turn = lax.div(lax.rem(tile, half), 2)
+
+    head = side * (pairs - 1)
+    lead = (pl.multiple_of(mine - side * pair, LANE), pair)
+    rest = (pl.multiple_of((1 - side) * (mine + pair), LANE), mine - pair)
+    home = (pl.multiple_of(side * mine, LANE), mine)
+    lead_wide = (pl.multiple_of(mine - side * pair - LANE, LANE), pair + 2 * LANE)
+    rest_wide = (pl.multiple_of((1 - side) * (mine + pair + LANE), LANE), mine - pair - LANE)
+    home_wide = (pl.multiple_of(side * (mine + LANE), LANE), mine - LANE)
+    every = (0, columns)
 
     def load(ref, buf, at, width, k):
         span = pl.ds(at, width)
@@ -74,13 +102,14 @@
         state_ref, s0.at[(pl.ds(1, levels),) + inner], load_sem.at[0]
     )
     fields = ((misfit_ref, misfit), (east_ref, east), (north_ref, north), (land_ref, land))
-    loads = [tracer] + [
-        load(ref, buf, first_at, first_width, 1 + k) for k, (ref, buf) in enumerate(fields)
+    loads = [
+        [load(ref, buf, *at, 1 + 4 * n + k) for k, (ref, buf) in enumerate(fields)]
+        for n, at in enumerate((lead_wide, rest_wide, home_wide))
     ]
-    later = [load(ref, buf, then_at, then_width, 5 + k) for k, (ref, buf) in enumerate(fields)]
-    small = [
-        pltpu.make_async_copy(matrix_ref, matrix, load_sem.at[9]),
-        pltpu.make_async_copy(select_ref, select, load_sem.at[10]),
+    loads[0].insert(0, tracer)
+    loads[2] += [
+        pltpu.make_async_copy(matrix_ref, matrix, load_sem.at[13]),
+        pltpu.make_async_copy(select_ref, select, load_sem.at[14]),
     ]
 
     barrier = pltpu.get_barrier_semaphore()
@@ -98,7 +127,7 @@
     def _():
         pl.semaphore_signal(barrier, inc=1, device_id=(grp + 1, tile), device_id_type=MESH)
 
-    for copy in loads + later + small:
+    for copy in loads[0] + loads[1] + loads[2]:
         copy.start()
 
     for buf in (s0, s1):
@@ -204,7 +233,7 @@
         for sends, _, copy in copies:
             pl.when(sends)(copy.wait_send)
 
-    def advance(src, dst, pad, first, count, row_first, row_count, at, width, edge=0):
+    def advance(src, dst, pad, first, count, row_first, row_count, at, width, edge=0, slot=0):
         if count <= 0 or row_count <= 0:
             return
         pieces = [(k, min(WIDTH, width - k)) for k in range(0, width, WIDTH)]
@@ -245,60 +274,76 @@
                 if pad:
                     dst[level + 1, middle, mid] = value
                 else:
-                    dst[level, rr, here] = value
-
-    def forward(first, count, row_first, row_count, far):
+                    dst[level - first + slot, rr, here] = value
+
+    def forward(first, count, chunk_list, far, same, since, begin=0, end=pairs):
         if count <= 0:
             return
-        here = lax.rem(tile, half)
-        base = (1 - side) * half if far else side * half
-        for r in range(row_first, row_first + row_count):
-            span = pl.ds(r * SUB, SUB)
-            target = pencil.at[pl.ds(tile * levels + first, count), span, :]
-
-            @pl.loop(0 if far else 1, half)
+        base = (1 - side if far else side) * half
+        base = base + (parity if same else 1 - parity)
+        mine_at = pl.ds(tile * levels + first, count)
+
+        def send(r, other, start, width):
+            source = s2.at[pl.ds(first, count), pl.ds(r * SUB, SUB), pl.ds(start, width)]
+            target = pencil.at[mine_at, pl.ds(r * SUB, SUB), :]
+            if r == uneven:
+                target = pencil_u.at[mine_at, :, pl.ds(0, width)]
+            if other is None:
+                pltpu.make_async_copy(source, target, fwd_recv.at[r]).start()
+            else:
+                pltpu.make_async_remote_copy(
+                    source, target, fwd_send, fwd_recv.at[r], (grp, other), MESH
+                ).start()
+
+        local = not far and same
+        for r in chunk_list:
+
+            @pl.loop(max(begin, 1) if local else begin, end)
             def _(i):
-                other = base + lax.rem(here + i, half)
-                cut = pl.ds(pl.multiple_of(other * part, LANE), part)
-                pltpu.make_async_remote_copy(
-                    s2.at[pl.ds(first, count), span, cut],
-                    target,
-                    fwd_send,
-                    fwd_recv.at[r],
-                    (grp, other),
-                    MESH,
-                ).start()
-
-            if not far:
-                own = pl.ds(pl.multiple_of(tile * part, LANE), part)
-                pltpu.make_async_copy(
-                    s2.at[pl.ds(first, count), span, own], target, fwd_recv.at[r]
-                ).start()
-
-    early = levels - 2 * near
-    inside = levels - 2
-    far_part, near_part = (far_at, mine), (near_at, mine)
-    first_part, then_part = (first_at, first_width), (then_at, then_width)
-    every = (0, columns)
-
-    for copy in loads:
-        copy.wait()
-    advance(s0, s1, True, 1, inside, 0, 1, *first_part, edge=-1)
-    advance(s0, s1, True, 1, inside, 1, chunks - 2, *first_part)
-    advance(s0, s1, True, 1, inside, chunks - 1, 1, *first_part, edge=1)
-    advance(s1, s2, False, near, early, 1, chunks - 2, *far_part)
-
-    pl.semaphore_wait(barrier, tiles - 1 + beside)
-
+                other = base + 2 * lax.rem(since + i, pairs)
+                if r == uneven:
+                    by_width(other, lambda width: send(r, other, uneven_start(other), width))
+                else:
+                    send(r, other, pl.multiple_of(other * part, LANE), part)
+
+            if local:
+                if r == uneven:
+                    by_width(tile, lambda width: send(r, None, uneven_start(tile), width))
+                else:
+                    send(r, None, pl.multiple_of(tile * part, LANE), part)
+
+    inner_chunks = list(range(1, chunks - 1))
+    outer_chunks = [0, chunks - 1]
+    all_chunks = inner_chunks + outer_chunks
     level0 = level_copies(s0, 0)
     row0 = row_copies(s0, 0, 0, 0, levels)
-    start(row0)
-    start(level0)
-    forward(near, early, 1, chunks - 2, True)
-
-    for copy in later + small:
+
+    def enter():
+        pl.semaphore_wait(barrier, tiles - 1 + beside)
+        start(level0)
+        start(row0)
+
+    def first_step(at, width):
+        advance(s0, s1, True, 1, inside, 0, 1, at, width, edge=-1)
+        advance(s0, s1, True, 1, inside, 1, chunks - 2, at, width)
+        advance(s0, s1, True, 1, inside, chunks - 1, 1, at, width, edge=1)
+
+    for copy in loads[0]:
         copy.wait()
-    advance(s0, s1, True, 1, inside, 1, chunks - 2, *then_part)
+    first_step(*lead_wide)
+    advance(s1, s2, False, near, early, 1, chunks - 2, *lead)
+    enter()
+    forward(0, early, inner_chunks, True, True, head, 0, 1)
+
+    for copy in loads[1]:
+        copy.wait()
+    first_step(*rest_wide)
+    advance(s1, s2, False, near, early, 1, chunks - 2, *rest)
+    forward(0, early, inner_chunks, True, True, head, 1, pairs)
+
+    for copy in loads[2]:
+        copy.wait()
+    advance(s0, s1, True, 1, inside, 1, chunks - 2, *home_wide)
     arrive(row0)
     advance(s0, s1, True, 1, inside, 0, 1, *every)
     advance(s0, s1, True, 1, inside, chunks - 1, 1, *every)
@@ -306,95 +351,175 @@
     row_mid = row_copies(s1, 1, 1, 1, levels - 2) if levels > 2 else []
     row_ends = row_copies(s1, 1, 2, 0, 1) + row_copies(s1, 1, 3, levels - 1, 1)
     start(row_mid)
-    advance(s1, s2, False, near, early, 1, chunks - 2, *near_part)
-    forward(near, early, 1, chunks - 2, False)
+    advance(s1, s2, False, near, early, 1, chunks - 2, *home)
+    arrive(row_mid)
+    for r in outer_chunks:
+        advance(s1, s2, False, near, early, r, 1, *every)
+
+    @pl.when(light)
+    def _():
+        forward(0, early, outer_chunks, True, True, turn)
 
     arrive(level0)
     advance(s0, s1, True, 0, 1, 0, chunks, *every)
     advance(s0, s1, True, levels - 1, 1, 0, chunks, *every)
     start(level1)
     start(row_ends)
-
-    arrive(row_mid)
-    for r in (0, chunks - 1):
-        advance(s1, s2, False, near, early, r, 1, *every)
-    for r in (0, chunks - 1):
-        forward(near, early, r, 1, True)
-        forward(near, early, r, 1, False)
-    advance(s1, s2, False, 1, near - 1, 0, chunks, *every)
-    advance(s1, s2, False, levels - near, near - 1, 0, chunks, *every)
-
-    size = tiles * levels * SUB
-    repeat = (
-        lax.shift_right_logical(lax.broadcasted_iota(jnp.int32, (size, tiles * levels), 0), 3)
-        == lax.broadcasted_iota(jnp.int32, (size, tiles * levels), 1)
-    ).astype(jnp.float32)
+    forward(0, early, inner_chunks, True, False, turn)
+
+    @pl.when(light)
+    def _():
+        forward(0, early, outer_chunks, True, False, turn)
+
+
+    advance(s1, s2, False, 1, near - 1, 0, chunks, *every, slot=early)
+    advance(s1, s2, False, levels - near, near - 1, 0, chunks, *every, slot=early + near - 1)
+    forward(early, 2 * near - 2, inner_chunks, True, True, turn)
+    forward(early, 2 * near - 2, inner_chunks, True, False, turn)
+
+    @pl.when(light)
+    def _():
+        forward(early, 2 * near - 2, outer_chunks, True, True, turn)
+        forward(early, 2 * near - 2, outer_chunks, True, False, turn)
+
+    forward(0, early, all_chunks, False, True, turn)
+    forward(early, 2 * near - 2, all_chunks, False, True, turn)
+
+    total = tiles * levels
+    size = total * SUB
+    row_of = lax.shift_right_logical(lax.broadcasted_iota(jnp.int32, (size, total), 0), 3)
+    level_of = lax.broadcasted_iota(jnp.int32, (size, total), 1)
+    repeat = (row_of == level_of).astype(jnp.float32)
+    in_tile = lax.rem(row_of, levels)
+    natural = jnp.where(
+        in_tile < early,
+        in_tile + near,
+        jnp.where(
+            in_tile < levels - 2,
+            1 + (in_tile - early) * (levels - 3),
+            (in_tile - (levels - 2)) * (levels - 1),
+        ),
+    )
+    pick = (row_of - in_tile + natural == level_of).astype(jnp.float32)
     tall = jnp.dot(repeat, matrix[...], precision=HIGHEST, preferred_element_type=jnp.float32)
     full = lax.dot_general(
         tall,
-        repeat,
+        pick,
         (((1,), (1,)), ((), ())),
         precision=HIGHEST,
         preferred_element_type=jnp.float32,
     )
-    same = (lax.broadcasted_iota(jnp.int32, (size, size), 0) & (SUB - 1)) == (
+    same_row = (lax.broadcasted_iota(jnp.int32, (size, size), 0) & (SUB - 1)) == (
         lax.broadcasted_iota(jnp.int32, (size, size), 1) & (SUB - 1)
     )
-    kron[...] = jnp.where(same, full, 0.0)
+    kron[...] = jnp.where(same_row, full, 0.0)
 
     arrive(level1)
     arrive(row_ends)
-    order = list(range(1, chunks - 1)) + [0, chunks - 1]
-    for r in order:
-        advance(s1, s2, False, 0, 1, r, 1, *every)
-        advance(s1, s2, False, levels - 1, 1, r, 1, *every)
-        for far in (True, False):
-            forward(0, near, r, 1, far)
-            forward(levels - near, near, r, 1, far)
-
-    for r in order:
+    for r in all_chunks:
+        advance(s1, s2, False, 0, 1, r, 1, *every, slot=levels - 2)
+        advance(s1, s2, False, levels - 1, 1, r, 1, *every, slot=levels - 1)
+        for same in (True, False):
+            if r in inner_chunks:
+                forward(levels - 2, 2, [r], True, same, turn)
+            else:
+                pl.when(light)(lambda: forward(levels - 2, 2, [r], True, same, turn))
+                pl.when(jnp.logical_not(light))(lambda: forward(0, levels, [r], True, same, turn))
+        forward(levels - 2, 2, [r], False, True, turn)
+        forward(0, levels, [r], False, False, turn)
+
+    def give(source, place):
+        def to(other):
+            pltpu.make_async_remote_copy(
+                source(other), place, ret_send, ret_recv, (grp, other), MESH
+            ).start()
+
+        @pl.loop(0, half)
+        def _(i):
+            to((1 - side) * half + i)
+
+        @pl.loop(1, half)
+        def _(i):
+            to(side * half + lax.rem(lax.rem(tile, half) + i, half))
+
+        pltpu.make_async_copy(source(tile), place, ret_recv).start()
+
+    def smoothed(block, width):
+        return jnp.dot(
+            kron[...],
+            block.reshape(size, width),
+            precision=HIGHEST,
+            preferred_element_type=jnp.float32,
+        )
+
+    def finish(r):
         span = pl.ds(r * SUB, SUB)
         chunk = pencil.at[:, span, :]
         pltpu.make_async_copy(chunk, chunk, fwd_recv.at[r]).wait()
-        result = jnp.dot(
-            kron[...],
-            pencil[:, r * SUB : (r + 1) * SUB, :].reshape(size, part),
-            precision=HIGHEST,
-            preferred_element_type=jnp.float32,
+        result = smoothed(pencil[:, r * SUB : (r + 1) * SUB, :], part)
+        smooth[:, r * SUB : (r + 1) * SUB, :] = result.reshape(tiles * levels, SUB, part)
+        give(
+            lambda other: smooth.at[pl.ds(other * levels, levels), span, :],
+            out_ref.at[:, span, pl.ds(pl.multiple_of(tile * part, LANE), part)],
         )
-        smooth[:, r * SUB : (r + 1) * SUB, :] = result.reshape(tiles * levels, SUB, part)
-        home = out_ref.at[:, span, pl.ds(pl.multiple_of(tile * part, LANE), part)]
-
-        def give(other):
-            pltpu.make_async_remote_copy(
-                smooth.at[pl.ds(other * levels, levels), span, :],
-                home,
-                ret_send,
-                ret_recv,
-                (grp, other),
-                MESH,
-            ).start()
-
-        @pl.loop(0, half)
-        def _(i):
-            give((1 - side) * half + i)
-
-        @pl.loop(1, half)
-        def _(i):
-            give(side * half + lax.rem(lax.rem(tile, half) + i, half))
-
-        pltpu.make_async_copy(
-            smooth.at[pl.ds(tile * levels, levels), span, :], home, ret_recv
-        ).start()
         surface_ref[r * SUB : (r + 1) * SUB, :] = (
             select[r * SUB : (r + 1) * SUB, :].astype(jnp.float32) * result[0:SUB]
         )
 
+    strip = pltpu.make_async_remote_copy(
+        smooth_u.at[0, :, pl.ds(pl.multiple_of((1 - side) * part, LANE), LANE)],
+        border,
+        border_sem.at[0],
+        border_sem.at[1],
+        (grp, partner),
+        MESH,
+    )
+
+    def finish_uneven(width):
+        span = pl.ds(uneven * SUB, SUB)
+        across = pl.ds(0, width)
+        chunk = pencil_u.at[:, :, across]
+        pltpu.make_async_copy(chunk, chunk, fwd_recv.at[uneven]).wait()
+        result = smoothed(pencil_u[:, :, 0:width], width)
+        smooth_u[:, :, 0:width] = result.reshape(tiles * levels, SUB, width)
+        give(
+            lambda other: smooth_u.at[pl.ds(other * levels, levels), :, across],
+            out_ref.at[:, span, pl.ds(uneven_start(tile), width)],
+        )
+        if width > part:
+            strip.start()
+            own = smooth_u[0, :, pl.ds(pl.multiple_of(side * LANE, LANE), part)]
+            surface_ref[span, :] = select[span, :].astype(jnp.float32) * own
+        else:
+            at = pl.ds(pl.multiple_of((1 - side) * LANE, LANE), width)
+            surface_ref[span, at] = select[span, at].astype(jnp.float32) * smooth_u[0, :, across]
+
+    for r in all_chunks:
+        if r == uneven:
+            by_width(tile, finish_uneven)
+        else:
+            finish(r)
+
+    def settle(width):
+        span = pl.ds(uneven * SUB, SUB)
+        if width > part:
+            strip.wait_send()
+        else:
+            strip.wait_recv()
+            at = pl.ds(pl.multiple_of(side * width, LANE), LANE)
+            surface_ref[span, at] = select[span, at].astype(jnp.float32) * border[...]
+        sent = s2.at[:, span, pl.ds(0, columns - width)]
+        pltpu.make_async_copy(sent, sent, fwd_send).wait()
+        returned = smooth_u.at[pl.ds(0, (tiles - 1) * levels), :, pl.ds(0, width)]
+        pltpu.make_async_copy(returned, returned, ret_send).wait()
+
+    by_width(tile, settle)
     for copies in (level0, row0, level1, row_mid, row_ends):
         leave(copies)
-    sent = s2.at[:, :, pl.ds(0, (tiles - 1) * part)]
+    even_rows = pl.ds(0, rows - SUB)
+    sent = s2.at[:, even_rows, pl.ds(0, (tiles - 1) * part)]
     pltpu.make_async_copy(sent, sent, fwd_send).wait()
-    returned = smooth.at[pl.ds(0, (tiles - 1) * levels)]
+    returned = smooth.at[pl.ds(0, (tiles - 1) * levels), even_rows]
     pltpu.make_async_copy(returned, returned, ret_send).wait()
     pltpu.make_async_copy(out_ref, out_ref, ret_recv).wait()
 
@@ -428,7 +553,10 @@
             pltpu.VMEM((total * SUB, total * SUB), jnp.float32),
             pltpu.VMEM((total, total), jnp.float32),
             pltpu.VMEM((rows, part), jnp.int32),
-            pltpu.SemaphoreType.DMA((11,)),
+            pltpu.VMEM((total, SUB, part + LANE), jnp.float32),
+            pltpu.VMEM((total, SUB, part + LANE), jnp.float32),
+            pltpu.VMEM((SUB, LANE), jnp.float32),
+            pltpu.SemaphoreType.DMA((15,)),
             pltpu.SemaphoreType.DMA((2, 2)),
             pltpu.SemaphoreType.DMA((2, 2)),
             pltpu.SemaphoreType.DMA((4, 2)),
@@ -437,6 +565,7 @@
             pltpu.SemaphoreType.DMA((rows // SUB,)),
             pltpu.SemaphoreType.DMA,
             pltpu.SemaphoreType.DMA,
+            pltpu.SemaphoreType.DMA((2,)),
         ],
         compiler_params=pltpu.CompilerParams(
             collective_id=0, has_side_effects=True, vmem_limit_bytes=40 * 1024 * 1024

time: 117 us -> 110 us (0.940); the launches traced: 115 us -> 110 us
  Pallas kernels: 113 us -> 107 us
    pallas_call x1, Pallas kernels: 113 us -> 107 us  [body(): pl.pallas_call(functools.partial(kernel, tiles, grps), out_shape=(pltpu.V...]
where the time goes in v1:
time: 110 us
  Pallas kernels  107 us (97%)
  local copies, waits for them, and re-layouts  1.94 us (2%)
    pallas_call x1, Pallas kernels, body(): pl.pallas_call(functools.partial(kernel, tiles, grps), out_shape=(pltpu.V...  107 us

profile of v1, /device:TPU:10, one launch (start us, length us, event | category | flops | bytes accessed | tf_op | source)
XLA Modules:
  0.0 109.9 jit_solution(13555588512732973807)
XLA Ops:
  0.6 107.3 %shard_map.86 = (f32[8,32,2048]{2,1,0:T(8,128)S(1)}, f32[32,256]{1,0:T(8,128)S(1)}) custom-call(f32[8,32,2048]{2,1,0:T(8,128)} %state_ref.1, f32[8,32,2048]{2,1,0:T(8,128)} %misfit_ref.1, f32[8,32,2048]{2,1,0:T(8,128)} %east_ref.1, f32[8,32,2048]{2,1,0:T(8,128)} %north_ref.1, s32[8,32,2048]{2,1,0:T(8,128)} %land_ref.1, s32[32,256]{1,0:T(8,128)} %select_ref.1, ...), custom_call_target="tpu_custom_call" | custom-call | tf_op jit(solution)/shard_map/pallas_call | solution.py:535
  108.0 1.3 %copy.11 = f32[8,32,2048]{2,1,0:T(8,128)} copy(f32[8,32,2048]{2,1,0:T(8,128)S(1)} %get-tuple-element.2) | data formatting | bytes 4194304
  109.3 0.6 copy.12

commit v2 on v1

--- a/solution.py
+++ b/solution.py
@@ -94,22 +94,41 @@
     home_wide = (pl.multiple_of(side * (mine + LANE), LANE), mine - LANE)
     every = (0, columns)
 
-    def load(ref, buf, at, width, k):
-        span = pl.ds(at, width)
-        return pltpu.make_async_copy(ref.at[:, :, span], buf.at[:, :, span], load_sem.at[k])
-
-    tracer = pltpu.make_async_copy(
-        state_ref, s0.at[(pl.ds(1, levels),) + inner], load_sem.at[0]
-    )
+    def state_load(at, width, k):
+        return pltpu.make_async_copy(
+            state_ref.at[:, :, pl.ds(at, width)],
+            s0.at[pl.ds(1, levels), pl.ds(SUB, rows), pl.ds(at + LANE, width)],
+            load_sem.at[k],
+        )
+
+    def field_loads(at, first, count, k):
+        span = (pl.ds(first, count), slice(None), pl.ds(*at))
+        return [
+            pltpu.make_async_copy(ref.at[span], buf.at[span], load_sem.at[k + n])
+            for n, (ref, buf) in enumerate(fields)
+        ]
+
     fields = ((misfit_ref, misfit), (east_ref, east), (north_ref, north), (land_ref, land))
     loads = [
-        [load(ref, buf, *at, 1 + 4 * n + k) for k, (ref, buf) in enumerate(fields)]
-        for n, at in enumerate((lead_wide, rest_wide, home_wide))
+        [state_load(pl.multiple_of(mine - side * pair - 2 * LANE, LANE), pair + 4 * LANE, 0)],
+        [
+            state_load(pl.multiple_of(side * (mine + 2 * LANE), LANE), mine - 2 * LANE, 1),
+            state_load(
+                pl.multiple_of((1 - side) * (mine + pair + 2 * LANE), LANE),
+                mine - pair - 2 * LANE,
+                2,
+            ),
+        ]
+        + field_loads(rest_wide, 0, levels, 3),
+        field_loads(home_wide, 0, levels, 7)
+        + field_loads(lead_wide, 0, 1, 11)
+        + field_loads(lead_wide, levels - 1, 1, 15),
     ]
-    loads[0].insert(0, tracer)
+    if inside > 0:
+        loads[0] += field_loads(lead_wide, 1, inside, 19)
     loads[2] += [
-        pltpu.make_async_copy(matrix_ref, matrix, load_sem.at[13]),
-        pltpu.make_async_copy(select_ref, select, load_sem.at[14]),
+        pltpu.make_async_copy(matrix_ref, matrix, load_sem.at[23]),
+        pltpu.make_async_copy(select_ref, select, load_sem.at[24]),
     ]
 
     barrier = pltpu.get_barrier_semaphore()
@@ -238,7 +257,7 @@
             return
         pieces = [(k, min(WIDTH, width - k)) for k in range(0, width, WIDTH)]
 
-        @pl.loop(0, count * row_count)
+        @pl.loop(0, count * row_count, unroll=2)
         def _(i):
             level = first + lax.div(i, row_count)
             row = pl.multiple_of((row_first + lax.rem(i, row_count)) * SUB, SUB)
@@ -330,9 +349,9 @@
 
     for copy in loads[0]:
         copy.wait()
+    enter()
     first_step(*lead_wide)
     advance(s1, s2, False, near, early, 1, chunks - 2, *lead)
-    enter()
     forward(0, early, inner_chunks, True, True, head, 0, 1)
 
     for copy in loads[1]:
@@ -524,6 +543,17 @@
     pltpu.make_async_copy(out_ref, out_ref, ret_recv).wait()
 
 
+def store(out_ref, surface_ref, out_hbm, surface_hbm, sem):
+    copies = [
+        pltpu.make_async_copy(out_ref, out_hbm, sem.at[0]),
+        pltpu.make_async_copy(surface_ref, surface_hbm, sem.at[1]),
+    ]
+    for copy in copies:
+        copy.start()
+    for copy in copies:
+        copy.wait()
+
+
 def body(tiles, grps, *args):
     levels, rows, columns = args[0].shape
     part = columns // tiles
@@ -532,7 +562,7 @@
     block = (levels, rows, columns)
     hbm = pl.BlockSpec(memory_space=pltpu.HBM)
     vmem = pl.BlockSpec(memory_space=pltpu.VMEM)
-    return pl.pallas_call(
+    held = pl.pallas_call(
         functools.partial(kernel, tiles, grps),
         out_shape=(
             pltpu.VMEM(block, jnp.float32),
@@ -556,7 +586,7 @@
             pltpu.VMEM((total, SUB, part + LANE), jnp.float32),
             pltpu.VMEM((total, SUB, part + LANE), jnp.float32),
             pltpu.VMEM((SUB, LANE), jnp.float32),
-            pltpu.SemaphoreType.DMA((15,)),
+            pltpu.SemaphoreType.DMA((25,)),
             pltpu.SemaphoreType.DMA((2, 2)),
             pltpu.SemaphoreType.DMA((2, 2)),
             pltpu.SemaphoreType.DMA((4, 2)),
@@ -571,6 +601,17 @@
             collective_id=0, has_side_effects=True, vmem_limit_bytes=40 * 1024 * 1024
         ),
     )(*[pltpu.with_memory_space_constraint(arg, pltpu.HBM) for arg in args])
+    return pl.pallas_call(
+        store,
+        out_shape=(
+            jax.ShapeDtypeStruct(block, jnp.float32),
+            jax.ShapeDtypeStruct((rows, part), jnp.float32),
+        ),
+        in_specs=[vmem] * 2,
+        out_specs=(hbm, hbm),
+        scratch_shapes=[pltpu.SemaphoreType.DMA((2,))],
+        compiler_params=pltpu.CompilerParams(vmem_limit_bytes=1024 * 1024),
+    )(*held)
 
 
 def solution(mesh):

time: 110 us -> 106 us (0.964)
  Pallas kernels: 107 us -> 105 us
  local copies, waits for them, and re-layouts: 1.94 us -> 0 us
    pallas_call x1, Pallas kernels: 107 us -> 103 us  [body(): pl.pallas_call(functools.partial(kernel, tiles, grps), out_shape=(pltpu.V...]
    unnamed x2 -> x0, local copies, waits for them, and re-layouts: 1.94 us -> none
    pallas_call x0 -> x1, Pallas kernels: none -> 1.34 us  [body(): pl.pallas_call(store, out_shape=(jax.ShapeDtypeStruct(block, jnp.float32)...]
where the time goes in v2:
time: 106 us; the launch traced here: 105 us
  Pallas kernels  105 us (99%)
    pallas_call x1, Pallas kernels, body(): pl.pallas_call(functools.partial(kernel, tiles, grps), out_shape=(pltpu.V...  103 us

profile of v2, /device:TPU:10, one launch (start us, length us, event | category | flops | bytes accessed | tf_op | source)
XLA Modules:
  0.0 105.4 jit_solution(6536424609468052712)
XLA Ops:
  0.6 103.5 %shard_map.86 = (f32[8,32,2048]{2,1,0:T(8,128)S(1)}, f32[32,256]{1,0:T(8,128)S(1)}) custom-call(f32[8,32,2048]{2,1,0:T(8,128)} %state_ref.1, f32[8,32,2048]{2,1,0:T(8,128)} %misfit_ref.1, f32[8,32,2048]{2,1,0:T(8,128)} %east_ref.1, f32[8,32,2048]{2,1,0:T(8,128)} %north_ref.1, s32[8,32,2048]{2,1,0:T(8,128)} %land_ref.1, s32[32,256]{1,0:T(8,128)} %select_ref.1, ...), custom_call_target="tpu_custom_call" | custom-call | tf_op jit(solution)/shard_map/pallas_call | solution.py:565
  104.1 1.3 %shard_map.87 = (f32[8,32,2048]{2,1,0:T(8,128)}, f32[32,256]{1,0:T(8,128)}) custom-call(f32[8,32,2048]{2,1,0:T(8,128)S(1)} %get-tuple-element.4.out_ref, f32[32,256]{1,0:T(8,128)S(1)} %get-tuple-element.5.surface_ref), custom_call_target="tpu_custom_call" | custom-call | tf_op jit(solution)/shard_map/pallas_call | solution.py:604

commit v3 on v2

--- a/solution.py
+++ b/solution.py
@@ -401,8 +401,6 @@
         forward(early, 2 * near - 2, outer_chunks, True, True, turn)
         forward(early, 2 * near - 2, outer_chunks, True, False, turn)
 
-    forward(0, early, all_chunks, False, True, turn)
-    forward(early, 2 * near - 2, all_chunks, False, True, turn)
 
     total = tiles * levels
     size = total * SUB
@@ -444,7 +442,7 @@
             else:
                 pl.when(light)(lambda: forward(levels - 2, 2, [r], True, same, turn))
                 pl.when(jnp.logical_not(light))(lambda: forward(0, levels, [r], True, same, turn))
-        forward(levels - 2, 2, [r], False, True, turn)
+        forward(0, levels, [r], False, True, turn)
         forward(0, levels, [r], False, False, turn)
 
     def give(source, place):
@@ -610,7 +608,7 @@
         in_specs=[vmem] * 2,
         out_specs=(hbm, hbm),
         scratch_shapes=[pltpu.SemaphoreType.DMA((2,))],
-        compiler_params=pltpu.CompilerParams(vmem_limit_bytes=1024 * 1024),
+        compiler_params=pltpu.CompilerParams(vmem_limit_bytes=1024 * 1024, skip_device_barrier=True),
     )(*held)
 
 

time: 106 us -> 106 us (level)
  no operation moved by 1% of the time
where the time goes in v3:
time: 106 us; the launch traced here: 105 us
  Pallas kernels  105 us (99%)
    pallas_call x1, Pallas kernels, body(): pl.pallas_call(functools.partial(kernel, tiles, grps), out_shape=(pltpu.V...  103 us

profile of v3, /device:TPU:10, one launch (start us, length us, event | category | flops | bytes accessed | tf_op | source)
XLA Modules:
  0.0 105.5 jit_solution(18032173703915830438)
XLA Ops:
  0.6 103.5 %shard_map.86 = (f32[8,32,2048]{2,1,0:T(8,128)S(1)}, f32[32,256]{1,0:T(8,128)S(1)}) custom-call(f32[8,32,2048]{2,1,0:T(8,128)} %state_ref.1, f32[8,32,2048]{2,1,0:T(8,128)} %misfit_ref.1, f32[8,32,2048]{2,1,0:T(8,128)} %east_ref.1, f32[8,32,2048]{2,1,0:T(8,128)} %north_ref.1, s32[8,32,2048]{2,1,0:T(8,128)} %land_ref.1, s32[32,256]{1,0:T(8,128)} %select_ref.1, ...), custom_call_target="tpu_custom_call" | custom-call | tf_op jit(solution)/shard_map/pallas_call | solution.py:563
  104.1 1.3 %shard_map.87 = (f32[8,32,2048]{2,1,0:T(8,128)}, f32[32,256]{1,0:T(8,128)}) custom-call(f32[8,32,2048]{2,1,0:T(8,128)S(1)} %get-tuple-element.4.out_ref, f32[32,256]{1,0:T(8,128)S(1)} %get-tuple-element.5.surface_ref), custom_call_target="tpu_custom_call" | custom-call | tf_op jit(solution)/shard_map/pallas_call | solution.py:602

commit v4 on v2

--- a/solution.py
+++ b/solution.py
@@ -51,6 +51,7 @@
     ret_send,
     ret_recv,
     border_sem,
+    joined,
 ):
     levels, rows, columns = state_ref.shape
     chunks = rows // SUB
@@ -83,6 +84,7 @@
     pairs = half // 2
     parity = lax.rem(tile, 2)
     light = parity == side
+    flip = parity
     turn = lax.div(lax.rem(tile, half), 2)
 
     head = side * (pairs - 1)
@@ -133,10 +135,18 @@
 
     barrier = pltpu.get_barrier_semaphore()
 
-    @pl.loop(1, tiles)
-    def _(i):
-        other = lax.rem(tile + i, tiles)
-        pl.semaphore_signal(barrier, inc=1, device_id=(grp, other), device_id_type=MESH)
+    late = tile >= tiles - 2
+
+    @pl.when(jnp.logical_not(late))
+    def _():
+        @pl.loop(1, tiles)
+        def _(i):
+            other = lax.rem(tile + i, tiles)
+            pl.semaphore_signal(barrier, inc=1, device_id=(grp, other), device_id_type=MESH)
+
+    @pl.when(late)
+    def _():
+        pl.semaphore_signal(barrier, inc=1, device_id=(grp, partner), device_id_type=MESH)
 
     @pl.when(grp > 0)
     def _():
@@ -252,12 +262,12 @@
         for sends, _, copy in copies:
             pl.when(sends)(copy.wait_send)
 
-    def advance(src, dst, pad, first, count, row_first, row_count, at, width, edge=0, slot=0):
+    def advance(src, dst, pad, first, count, row_first, row_count, at, width, edge=0, slot=0, unroll=2):
         if count <= 0 or row_count <= 0:
             return
         pieces = [(k, min(WIDTH, width - k)) for k in range(0, width, WIDTH)]
 
-        @pl.loop(0, count * row_count, unroll=2)
+        @pl.loop(0, count * row_count, unroll=unroll)
         def _(i):
             level = first + lax.div(i, row_count)
             row = pl.multiple_of((row_first + lax.rem(i, row_count)) * SUB, SUB)
@@ -338,8 +348,16 @@
     row0 = row_copies(s0, 0, 0, 0, levels)
 
     def enter():
-        pl.semaphore_wait(barrier, tiles - 1 + beside)
-        start(level0)
+        pl.semaphore_wait(barrier, jnp.where(late, tiles - 1, tiles - 3) + beside)
+
+        @pl.when(late)
+        def _():
+            @pl.loop(0, tiles - 2)
+            def _(other):
+                pl.semaphore_signal(joined, inc=1, device_id=(grp, other), device_id_type=MESH)
+
+        sends, _, up = level0[1]
+        start([level0[0], (sends & (tile != tiles - 3), None, up)])
         start(row0)
 
     def first_step(at, width):
@@ -347,12 +365,26 @@
         advance(s0, s1, True, 1, inside, 1, chunks - 2, at, width)
         advance(s0, s1, True, 1, inside, chunks - 1, 1, at, width, edge=1)
 
+    enter()
     for copy in loads[0]:
         copy.wait()
-    enter()
-    first_step(*lead_wide)
-    advance(s1, s2, False, near, early, 1, chunks - 2, *lead)
-    forward(0, early, inner_chunks, True, True, head, 0, 1)
+
+    @pl.when(tile == tiles - 3)
+    def _():
+        pl.semaphore_wait(joined, 2)
+        level0[1][2].start()
+
+    advance(s0, s1, True, 1, inside, 0, 1, *lead_wide, edge=-1, unroll=3)
+    advance(s0, s1, True, 1, inside, 1, chunks - 2, *lead_wide, unroll=3)
+    advance(s1, s2, False, near, early, 1, chunks - 3, *lead)
+    forward(0, early, inner_chunks[:-1], True, True, head, 0, 1)
+    advance(s0, s1, True, 1, inside, chunks - 1, 1, *lead_wide, edge=1, unroll=3)
+    advance(s1, s2, False, near, early, chunks - 2, 1, *lead)
+    forward(0, early, inner_chunks[-1:], True, True, head, 0, 1)
+
+    @pl.when(tile < tiles - 3)
+    def _():
+        pl.semaphore_wait(joined, 2)
 
     for copy in loads[1]:
         copy.wait()
@@ -455,7 +487,7 @@
 
         @pl.loop(0, half)
         def _(i):
-            to((1 - side) * half + i)
+            to((1 - side) * half + i - lax.rem(i, 2) + lax.rem(i + flip, 2))
 
         @pl.loop(1, half)
         def _(i):
@@ -596,6 +628,7 @@
             pltpu.SemaphoreType.DMA,
             pltpu.SemaphoreType.DMA,
             pltpu.SemaphoreType.DMA((2,)),
+            pltpu.SemaphoreType.REGULAR,
         ],
         compiler_params=pltpu.CompilerParams(
             collective_id=0, has_side_effects=True, vmem_limit_bytes=40 * 1024 * 1024

time: 106 us -> 106 us (level)
  no operation moved by 1% of the time
where the time goes in v4:
time: 106 us; the launch traced here: 105 us
  Pallas kernels  105 us (99%)
    pallas_call x1, Pallas kernels, body(): pl.pallas_call(functools.partial(kernel, tiles, grps), out_shape=(pltpu.V...  103 us

profile of v4, /device:TPU:10, one launch (start us, length us, event | category | flops | bytes accessed | tf_op | source)
XLA Modules:
  0.0 105.3 jit_solution(9112364612342164047)
XLA Ops:
  0.6 103.3 %shard_map.86 = (f32[8,32,2048]{2,1,0:T(8,128)S(1)}, f32[32,256]{1,0:T(8,128)S(1)}) custom-call(f32[8,32,2048]{2,1,0:T(8,128)} %state_ref.1, f32[8,32,2048]{2,1,0:T(8,128)} %misfit_ref.1, f32[8,32,2048]{2,1,0:T(8,128)} %east_ref.1, f32[8,32,2048]{2,1,0:T(8,128)} %north_ref.1, s32[8,32,2048]{2,1,0:T(8,128)} %land_ref.1, s32[32,256]{1,0:T(8,128)} %select_ref.1, ...), custom_call_target="tpu_custom_call" | custom-call | tf_op jit(solution)/shard_map/pallas_call | solution.py:597
  104.0 1.3 %shard_map.87 = (f32[8,32,2048]{2,1,0:T(8,128)}, f32[32,256]{1,0:T(8,128)}) custom-call(f32[8,32,2048]{2,1,0:T(8,128)S(1)} %get-tuple-element.4.out_ref, f32[32,256]{1,0:T(8,128)S(1)} %get-tuple-element.5.surface_ref), custom_call_target="tpu_custom_call" | custom-call | tf_op jit(solution)/shard_map/pallas_call | solution.py:637

commit v5 on v2

--- a/solution.py
+++ b/solution.py
@@ -610,7 +610,7 @@
         in_specs=[vmem] * 2,
         out_specs=(hbm, hbm),
         scratch_shapes=[pltpu.SemaphoreType.DMA((2,))],
-        compiler_params=pltpu.CompilerParams(vmem_limit_bytes=1024 * 1024),
+        compiler_params=pltpu.CompilerParams(vmem_limit_bytes=1024 * 1024, skip_device_barrier=True),
     )(*held)
 
 

time: 106 us -> 106 us (level)
  no operation moved by 1% of the time
where the time goes in v5:
time: 106 us; the launch traced here: 105 us
  Pallas kernels  105 us (99%)
    pallas_call x1, Pallas kernels, body(): pl.pallas_call(functools.partial(kernel, tiles, grps), out_shape=(pltpu.V...  103 us

profile of v5, /device:TPU:10, one launch (start us, length us, event | category | flops | bytes accessed | tf_op | source)
XLA Modules:
  0.0 105.4 jit_solution(6536424609468052712)
XLA Ops:
  0.6 103.5 %shard_map.86 = (f32[8,32,2048]{2,1,0:T(8,128)S(1)}, f32[32,256]{1,0:T(8,128)S(1)}) custom-call(f32[8,32,2048]{2,1,0:T(8,128)} %state_ref.1, f32[8,32,2048]{2,1,0:T(8,128)} %misfit_ref.1, f32[8,32,2048]{2,1,0:T(8,128)} %east_ref.1, f32[8,32,2048]{2,1,0:T(8,128)} %north_ref.1, s32[8,32,2048]{2,1,0:T(8,128)} %land_ref.1, s32[32,256]{1,0:T(8,128)} %select_ref.1, ...), custom_call_target="tpu_custom_call" | custom-call | tf_op jit(solution)/shard_map/pallas_call | solution.py:565
  104.1 1.3 %shard_map.87 = (f32[8,32,2048]{2,1,0:T(8,128)}, f32[32,256]{1,0:T(8,128)}) custom-call(f32[8,32,2048]{2,1,0:T(8,128)S(1)} %get-tuple-element.4.out_ref, f32[32,256]{1,0:T(8,128)S(1)} %get-tuple-element.5.surface_ref), custom_call_target="tpu_custom_call" | custom-call | tf_op jit(solution)/shard_map/pallas_call | solution.py:604
